TPU v7x, 32 devices: a whole 2x2x4 slice. The times are simulated.
32 devices in a mesh: grp: 2 (over x), roll: 8 (over z, y), head: 2 (over core).
Axes of the slice: x: 2, y: 2, z: 4, core: 2. Of those that a mesh axis runs over, the one named last changes fastest.
Arguments:
- store: bfloat16 [8, 1024, 576], P('grp', 'roll'), parts along dimension 0, may hold values from -7 to 7
- queries: bfloat16 [2, 128, 12288], P(None, ('grp', 'roll'), 'head'), parts along dimension 1, may hold values from -7.5 to 7.5
- table: bfloat16 [8192, 576], P('roll'), may hold values from -6 to 6
- w_uk: bfloat16 [64, 128, 512], P('head'), may hold values from -0.5 to 0.5
- w_uv: bfloat16 [64, 512, 128], P('head'), may hold values from -1.796875 to 1.796875
- w_out: bfloat16 [8192, 7168], P('head', 'roll'), may hold values from -0.0625 to 0.0625
- counts: int32 [8], P('grp'), parts along dimension 0, may hold values from 4 to 32, as said below
- prompt_rows: int32 [8], P('grp'), parts along dimension 0, may hold values from 0 to 3, each once
- decode_perm: int32 [16], P('grp'), parts along dimension 0, may hold values from 0 to 7, each once
- token_ids: int32 [128, 2], P('grp'), parts along dimension 0, may hold values from 0 to 8191
Outputs:
- layer_out: bfloat16 [128, 2, 7168], P(('grp', 'head'), None, 'roll'), parts along dimension 0
There are 2 independent parts, one for each index of `grp`. A program takes and returns all parts, laid end to end along the dimension named above; an argument that names none is the same for every part. Nothing has to cross between parts.
Inputs may be any that keep to these rules, and one draw needn't show every extreme that they name: The counts sum to 64; every aligned block of 8 consecutive samples covers at most 3 prompts, and some block covers exactly 3.
All inputs are finite; a program needn't handle non-finite values.
Results may differ from a plain program's by a relative error of at most 0.008.
Values may be sent and summed in bfloat16 or wider, within the bound.
A program may use at most 128 MiB of HBM per device.

v0:
```python
import jax
import jax.numpy as jnp
from jax import lax
from jax.sharding import PartitionSpec as P

KV_RANK = 512
ROPE_DIM = 64
NOPE_DIM = 128


masked_fill = -1e30
rope_base = 10000.0


def pick_values(values, positions):
    matches = positions[..., None] == jnp.arange(values.shape[0], dtype=jnp.int32)
    return jnp.sum(jnp.where(matches, values, 0), axis=-1)


def rotate_rope(latent_rows, positions):
    half_dim = ROPE_DIM // 2
    freqs = rope_base ** (-jnp.arange(half_dim, dtype=jnp.float32) / half_dim)
    angles = positions[:, None] * freqs[None, :]
    cosine = jnp.cos(angles)
    sine = jnp.sin(angles)
    front = latent_rows[..., KV_RANK : KV_RANK + half_dim]
    behind = latent_rows[..., KV_RANK + half_dim :]
    return jnp.concatenate(
        [
            latent_rows[..., :KV_RANK],
            front * cosine - behind * sine,
            front * sine + behind * cosine,
        ],
        axis=-1,
    )


def shards(store, queries, table, w_uk, w_uv, w_out, counts, prompt_rows, decode_perm, token_ids):
    roll_count = lax.axis_size("roll")
    roll_index = lax.axis_index("roll")
    step_count = queries.shape[0]
    slots_dev = queries.shape[1]
    latent_width = store.shape[2]
    cache_len = store.shape[1] * roll_count
    bound_ends = jnp.cumsum(counts)
    sample_ids = jnp.arange(roll_count * slots_dev, dtype=jnp.int32)
    prompt_of = jnp.sum((bound_ends[None, :] <= sample_ids[:, None]).astype(jnp.int32), axis=1)
    devices = jnp.arange(roll_count, dtype=jnp.int32)
    block_of = jnp.sum(
        jnp.where(decode_perm[None, :] == devices[:, None], devices[None, :], 0), axis=1
    )
    slot_offsets = jnp.arange(slots_dev, dtype=jnp.int32)
    slot_prompt = pick_values(prompt_of, block_of[:, None] * slots_dev + slot_offsets[None, :])
    send_rows = pick_values(prompt_rows, slot_prompt).reshape(-1)
    outgoing = jnp.take(store, send_rows, axis=0).reshape(
        roll_count, slots_dev, store.shape[1], latent_width
    )
    incoming = lax.all_to_all(outgoing, "roll", split_axis=0, concat_axis=2, tiled=True)
    cache_rows = incoming.reshape(slots_dev, cache_len, latent_width)
    flat_ids = token_ids.reshape(-1)
    vocab_dev = table.shape[0]
    vocab_base = roll_index * vocab_dev
    one_hot = (
        flat_ids[:, None] - vocab_base == jnp.arange(vocab_dev, dtype=jnp.int32)[None, :]
    ).astype(jnp.bfloat16)
    looked = lax.psum_scatter(
        jnp.dot(one_hot, table, preferred_element_type=jnp.float32),
        "roll",
        scatter_dimension=0,
        tiled=True,
    )
    looked = (
        looked.astype(jnp.bfloat16).astype(jnp.float32).reshape(slots_dev, step_count, latent_width)
    )
    positions = (cache_len + jnp.arange(step_count)).astype(jnp.float32)
    new_latents = rotate_rope(looked, positions).astype(jnp.bfloat16)
    head_count = w_uk.shape[0]
    query_parts = queries.reshape(step_count, slots_dev, head_count, -1)
    q_latent = jnp.einsum(
        "tshd,hdc->tshc", query_parts[..., :NOPE_DIM], w_uk, preferred_element_type=jnp.float32
    ).astype(jnp.bfloat16)
    q_full = jnp.concatenate([q_latent, query_parts[..., NOPE_DIM:]], axis=-1)
    score_scale = (NOPE_DIM + ROPE_DIM) ** (-0.5)
    cache_scores = (
        jnp.einsum("tshc,sjc->tshj", q_full, cache_rows, preferred_element_type=jnp.float32)
        * score_scale
    )
    new_scores = (
        jnp.einsum("tshc,suc->tshu", q_full, new_latents, preferred_element_type=jnp.float32)
        * score_scale
    )
    allowed = jnp.arange(step_count)[None, :] <= jnp.arange(step_count)[:, None]
    new_scores = jnp.where(allowed[:, None, None, :], new_scores, masked_fill)
    row_max = jnp.maximum(jnp.max(cache_scores, axis=-1), jnp.max(new_scores, axis=-1))[..., None]
    cache_exp = jnp.exp(cache_scores - row_max)
    new_exp = jnp.exp(new_scores - row_max)
    denom = jnp.sum(cache_exp, axis=-1, keepdims=True) + jnp.sum(new_exp, axis=-1, keepdims=True)
    cache_probs = (cache_exp / denom).astype(jnp.bfloat16)
    new_probs = (new_exp / denom).astype(jnp.bfloat16)
    attended = jnp.einsum(
        "tshj,sjc->tshc", cache_probs, cache_rows[..., :KV_RANK], preferred_element_type=jnp.float32
    )
    attended = attended + jnp.einsum(
        "tshu,suc->tshc", new_probs, new_latents[..., :KV_RANK], preferred_element_type=jnp.float32
    )
    attended = attended.astype(jnp.bfloat16)
    head_out = jnp.einsum(
        "tshc,hcv->tshv", attended, w_uv, preferred_element_type=jnp.float32
    ).astype(jnp.bfloat16)
    slot_major = head_out.transpose(1, 0, 2, 3).reshape(slots_dev * step_count, -1)
    partial_out = jnp.dot(
        lax.all_gather(slot_major, "roll", axis=0, tiled=True),
        w_out,
        preferred_element_type=jnp.float32,
    )
    summed = lax.psum_scatter(partial_out, "head", scatter_dimension=0, tiled=True)
    return summed.astype(jnp.bfloat16).reshape(-1, step_count, w_out.shape[1])


def solution(mesh):
    in_specs = (
        P("grp", "roll", None),
        P(None, ("grp", "roll"), "head"),
        P("roll", None),
        P("head", None, None),
        P("head", None, None),
        P("head", "roll"),
        P("grp"),
        P("grp"),
        P("grp"),
        P("grp", None),
    )
    out_specs = P(("grp", "head"), None, "roll")
    return jax.shard_map(shards, mesh=mesh, in_specs=in_specs, out_specs=out_specs, check_vma=False)
```

profile of v0, /device:TPU:0, one launch (start us, length us, event | category | flops | bytes accessed | tf_op | source)
XLA Modules:
  0.0 362.8 jit_solution(11651693616669206604)
XLA Ops:
  6.5 0.9 reduce-window.8
  7.5 0.8 select_reduce_fusion.2
  8.7 0.7 select_reduce_fusion.1
  9.5 7.1 %gather_fusion = bf16[64,128,576]{1,2,0:T(8,128)(2,1)} fusion(bf16[4,128,576]{1,2,0:T(8,128)(2,1)} %param.10, s32[1024]{0:T(1024)S(1)} %pad_clamp_fusion), kind=kCustom, calls=%fused_computation | custom fusion | bytes 18874624 | tf_op jit(solution)/shard_map/jit(_take)/gather | solution.py:55
  16.6 8.3 %broadcast_select_fusion = bf16[8,8,128,576]{2,3,1,0:T(8,128)(2,1)} fusion(bf16[8,8,128,576]{2,3,1,0:T(8,128)(2,1)} %bitcast.87, pred[8,8]{1,0:T(8,128)(4,1)S(1)} %compare_and_fusion), kind=kLoop, calls=%fused_computation.3 | loop fusion | flops 4718592 | bytes 18874432 | tf_op jit(solution)/shard_map/jit(_take)/select_n | solution.py:55
  24.9 7.4 %all-to-all-start = ((bf16[8,8,128,576]{2,3,1,0:T(8,128)(2,1)}), bf16[8,8,128,576]{2,3,1,0:T(8,128)(2,1)}, u32[]{:S(2)}, u32[]{:S(2)}) async-start(bf16[8,8,128,576]{2,3,1,0:T(8,128)(2,1)} %broadcast_select_fusion), calls=%async_computation | async-start | bytes 18874368 | tf_op jit(solution)/shard_map/all_to_all | solution.py:58
  32.7 1.3 fusion.25
  34.5 2.8 fusion.9
  37.5 208.2 %reduce-scatter.3.cloned.1.call-done = f32[16,576]{1,0:T(8,128)} async-done(((f32[128,576]{1,0:T(8,128)}), f32[16,576]{1,0:T(8,128)}) %reduce-scatter.3.cloned.1.call-update) | async-done | bytes 36880 | tf_op jit(solution)/shard_map/reduce_scatter | solution.py:66
  245.7 0.8 convert_element_type.53
  246.6 0.6 fusion.39
  247.3 13.4 %copy.33 = bf16[1,8,8,128,576]{3,2,4,1,0:T(8,128)(2,1)} copy(bf16[1,8,8,128,576]{3,4,1,2,0:T(8,128)(2,1)} %bitcast.5) | data formatting | bytes 18874368 | tf_op jit(solution)/shard_map/all_to_all | solution.py:58
  260.7 14.8 %reshape.225 = bf16[8,1024,576,1]{1,2,0,3:T(8,128)(2,1)} reshape(bf16[1,8,8,128,576]{3,2,4,1,0:T(8,128)(2,1)} %copy.33) | data formatting | bytes 18874368 | tf_op jit(solution)/shard_map/reshape | solution.py:59
  275.5 14.9 %reshape.209 = bf16[8,1024,576]{1,2,0:T(8,128)(2,1)} reshape(bf16[1,8,8,128,576]{3,2,4,1,0:T(8,128)(2,1)} %copy.33) | data formatting | bytes 18874368 | tf_op jit(solution)/shard_map/reshape | solution.py:59
  290.4 5.8 %bitcast_reduce_fusion = (f32[2,8,32]{2,0,1:T(2,128)S(1)}, f32[8,1024,2,32]{1,3,2,0:T(8,128)S(1)}) fusion(bf16[2,8,32,576]{3,1,0,2:T(8,128)(2,1)S(1)} %pad_maximum_fusion, bf16[8,1024,576,1]{1,2,0,3:T(8,128)(2,1)} %reshape.225), kind=kOutput, calls=%fused_computation.9 | convolution fusion | flops 605027840 | bytes 12126208 | tf_op jit(solution)/shard_map/tshc,sjc->tshj/dot_general | solution.py:85
  296.3 0.5 fusion.6
  296.9 2.9 fusion.2
  300.1 3.0 fusion.14
  303.1 0.7 copy.65
  303.9 38.4 %all-gather.2.cloned.1.call-done = bf16[128,4096]{1,0:T(8,128)(2,1)} async-done(((bf16[16,4096]{1,0:T(8,128)(2,1)}), bf16[128,4096]{1,0:T(8,128)(2,1)}) %all-gather.2.cloned.1.call-update) | async-done | bytes 1048592 | tf_op jit(solution)/shard_map/all_gather | solution.py:112
  342.3 5.5 %fusion.40 = f32[128,896]{1,0:T(8,128)} fusion(bf16[128,4096]{1,0:T(8,128)(2,1)} %all-gather.2.cloned.1.call-done, bf16[4096,896]{1,0:T(8,128)(2,1)} %param.15), kind=kOutput, calls=%fused_computation.74 | convolution fusion | flops 939524096 | bytes 8847360 | tf_op jit(solution)/shard_map/dot_general | solution.py:111
  347.9 6.8 %reduce-scatter.5.cloned.1.call-done = f32[64,896]{1,0:T(8,128)} async-done(((f32[128,896]{1,0:T(8,128)}), f32[64,896]{1,0:T(8,128)}) %reduce-scatter.5.cloned.1.call-update) | async-done | bytes 229392 | tf_op jit(solution)/shard_map/reduce_scatter | solution.py:116
  354.7 1.0 convert_element_type.61
  355.6 0.7 reshape.214
  (46 shorter events, 2.2 us)
Async XLA Ops:
  6.5 26.1 %copy-start = (bf16[1024,576]{0,1:T(8,128)(2,1)S(1)}, bf16[1024,576]{0,1:T(8,128)(2,1)}, u32[]{:S(2)}) copy-start(bf16[1024,576]{0,1:T(8,128)(2,1)} %param.12) | copy-start | bytes 3538948
  24.9 7.5 %copy-start.4 = (s32[64,2]{0,1:T(2,128)S(1)}, s32[64,2]{0,1:T(2,128)}, u32[]{:S(2)}) copy-start(s32[64,2]{0,1:T(2,128)} %param.19) | copy-start | bytes 1540
  24.9 9.1 %copy-start.3 = (bf16[2,8,6144]{2,1,0:T(8,128)(2,1)S(1)}, bf16[2,8,6144]{2,1,0:T(8,128)(2,1)}, u32[]{:S(2)}) copy-start(bf16[2,8,6144]{2,1,0:T(8,128)(2,1)} %param.11) | copy-start | bytes 589828
  24.9 222.4 %all-to-all-start = ((bf16[8,8,128,576]{2,3,1,0:T(8,128)(2,1)}), bf16[8,8,128,576]{2,3,1,0:T(8,128)(2,1)}, u32[]{:S(2)}, u32[]{:S(2)}) async-start(bf16[8,8,128,576]{2,3,1,0:T(8,128)(2,1)} %broadcast_select_fusion), calls=%async_computation | async-start | bytes 18874368 | tf_op jit(solution)/shard_map/all_to_all | solution.py:58
  32.3 213.4 %reduce-scatter.3.cloned.1.call-start = ((), (), s32[]{:S(2)}) async-start(), calls=%async_computation.3 | async-start | bytes 368640 | tf_op jit(solution)/shard_map/reduce_scatter | solution.py:66
  34.0 308.3 %all-gather.2.cloned.1.call-start = ((), (), s32[]{:S(2)}) async-start(), calls=%async_computation.4 | async-start | bytes 1179648 | tf_op jit(solution)/shard_map/all_gather | solution.py:112
  290.4 6.5 %copy-start.2 = (bf16[8,1024,576]{1,2,0:T(8,128)(2,1)S(1)}, bf16[8,1024,576]{1,2,0:T(8,128)(2,1)}, u32[]{:S(2)}) copy-start(bf16[8,1024,576]{1,2,0:T(8,128)(2,1)} %reshape.209) | copy-start | bytes 28311556
  303.9 50.8 %reduce-scatter.5.cloned.1.call-start = ((), (), s32[]{:S(2)}) async-start(), calls=%async_computation.5 | async-start | bytes 688128 | tf_op jit(solution)/shard_map/reduce_scatter | solution.py:116
  342.3 14.0 %copy-start.1 = (bf16[1024,576]{0,1:T(8,128)(2,1)S(1)}, bf16[1024,576]{0,1:T(8,128)(2,1)}, u32[]{:S(2)}) copy-start(bf16[1024,576]{0,1:T(8,128)(2,1)} %param.12) | copy-start | bytes 3538948
Sparse Core Ops, SparseCore 0:
  36.4 209.2 reduce-scatter.2
  304.0 38.2 all-gather.1
  348.0 6.5 reduce-scatter.4
where the time goes:
time: 364 us; the launch traced here: 363 us
  waiting for transfers between devices  253 us (70%)
  local copies, waits for them, and re-layouts  52.4 us (14%)
  matrix products  22.4 us (6%)
  other arithmetic  13.8 us (4%)
  between operations  13.3 us (4%)
  starting transfers between devices  7.53 us (2%)
    reduce_scatter x1, waiting for transfers between devices, shards(): lax.psum_scatter(jnp.dot(one_hot, table, preferred_element_type=jnp.float...  208 us
    all_gather x1, waiting for transfers between devices, shards(): lax.all_gather(slot_major, 'roll', axis=0, tiled=True)  38.4 us
    reshape x2, local copies, waits for them, and re-layouts, shards(): cache_rows = incoming.reshape(slots_dev, cache_len, latent_width)  29.7 us
    all_to_all x1, local copies, waits for them, and re-layouts, shards(): lax.all_to_all(outgoing, 'roll', split_axis=0, concat_axis=2, tiled=True)  13.4 us
    select_n x2, other arithmetic, shards(): jnp.take(store, send_rows, axis=0)  8.31 us
    all_to_all x1, starting transfers between devices, shards(): lax.all_to_all(outgoing, 'roll', split_axis=0, concat_axis=2, tiled=True)  7.41 us
  transfers between devices with their start and end apart: 4, of which 3 were waited for; matrix products, arithmetic and copies ran while one was open for 2% of the time, Pallas kernels for 0%

commit v1 on v0

--- a/solution.py
+++ b/solution.py
@@ -1,6 +1,11 @@
+import functools
+
 import jax
 import jax.numpy as jnp
+import numpy as np
 from jax import lax
+from jax.experimental import pallas as pl
+from jax.experimental.pallas import tpu as pltpu
 from jax.sharding import PartitionSpec as P
 
 KV_RANK = 512
@@ -117,7 +122,397 @@
     return summed.astype(jnp.bfloat16).reshape(-1, step_count, w_out.shape[1])
 
 
+def contract_last(a, b):
+    return lax.dot_general(a, b, (((1,), (1,)), ((), ())), preferred_element_type=jnp.float32)
+
+
+def fused_kernel(
+    counts, prompt_rows, decode_perm, token_ids, rope_cos, rope_sin, queries, store, table, w_uk, w_uv, w_out,
+    out,
+    kv, table_v, uk_v, uv_v, wout_v, contrib, tokens, new_keys, q_all, row_of, m_ref, l_ref, acc, att, heads_all, part, other,
+    load_sem, kv_recv, own_send, z_send, y_send, sib_send, tok_recv, tok_send,
+    ho_recv, ho_own_send, ho_z_send, ho_y_send, ex_sem,
+):
+    me = lax.axis_index("roll")
+    core = lax.axis_index("head")
+    z, y = me // 2, me % 2
+    flip = 1 - y
+    prompts = store.shape[0]
+    half = prompts // 2
+    block = store.shape[1]
+    head_count = uk_v.shape[0]
+    last = 3
+
+    def to(roll):
+        return {"roll": roll}
+
+    sibling = {"head": 1 - core}
+    mine = pl.ds(half * core, half)
+
+    def remote(src, dst, send, recv, device):
+        return pltpu.make_async_remote_copy(
+            src_ref=src, dst_ref=dst, send_sem=send, recv_sem=recv, device_id=device,
+            device_id_type=pl.DeviceIdType.MESH,
+        )
+
+    loads = [
+        pltpu.make_async_copy(table, table_v, load_sem.at[0]),
+        pltpu.make_async_copy(w_uk, uk_v, load_sem.at[1]),
+        pltpu.make_async_copy(store, kv.at[me], load_sem.at[2]),
+        pltpu.make_async_copy(w_uv, uv_v, load_sem.at[3]),
+        pltpu.make_async_copy(w_out, wout_v, load_sem.at[4]),
+    ]
+    for load in loads:
+        load.start()
+
+    barrier = pltpu.get_barrier_semaphore()
+    for k in range(1, 8):
+        pl.semaphore_signal(barrier, inc=1, device_id=to((me + k) % 8), device_id_type=pl.DeviceIdType.MESH)
+    pl.semaphore_signal(barrier, inc=1, device_id=sibling, device_id_type=pl.DeviceIdType.MESH)
+    pl.semaphore_wait(barrier, 8)
+
+    near = jnp.minimum(z, last - z)
+
+    def layer(i):
+        up = jnp.where(i == 0, near, jnp.where(i > near, i, i - 1))
+        return jnp.where(z <= 1, up, last - up)
+
+    own_block = store.at[mine]
+
+    def own_copy(step):
+        slot = 0 if step < 0 else 1
+        return remote(own_block, kv.at[me, mine], own_send.at[slot], kv_recv.at[me, core], to(me + 2 * step))
+
+    def z_copy(i):
+        src = layer(i) * 2 + y
+        step = jnp.where(layer(i) < z, 2, -2)
+        return remote(kv.at[src, mine], kv.at[src, mine], z_send.at[i], kv_recv.at[src, core], to(me + step))
+
+    def z_goes_on(i):
+        return jnp.where(layer(i) < z, z < last, z > 0)
+
+    def y_copy(i):
+        src = layer(i) * 2 + y
+        return remote(kv.at[src, mine], kv.at[src, mine], y_send.at[i], kv_recv.at[src, core], to(z * 2 + flip))
+
+    def own_y_copy():
+        return remote(own_block, kv.at[me, mine], y_send.at[0], kv_recv.at[me, core], to(z * 2 + flip))
+
+    def sib_copy(i, side):
+        src = layer(i) * 2 + side
+        return remote(kv.at[src, mine], kv.at[src, mine], sib_send.at[i, side], kv_recv.at[src, core], sibling)
+
+    def await_block(src, which):
+        ref = kv.at[src, pl.ds(half * which, half)]
+        pltpu.make_async_copy(ref, ref, kv_recv.at[src, which]).wait()
+
+    own_y_copy().start()
+
+    @pl.when(z < last)
+    def _():
+        own_copy(1).start()
+
+    @pl.when(z > 0)
+    def _():
+        own_copy(-1).start()
+
+    loads[0].wait()
+    rows_here = table_v.shape[0]
+    spots = lax.broadcasted_iota(jnp.int32, (token_ids.shape[0], rows_here), 1) + me * rows_here
+    picked = []
+    for t in range(2):
+        hot = jnp.where(token_ids[:, t : t + 1] == spots, 1.0, 0.0).astype(jnp.bfloat16)
+        got = jnp.dot(hot, table_v[...], preferred_element_type=jnp.float32)
+        picked.append(got.reshape(8, 8, got.shape[-1]))
+    contrib[...] = jnp.concatenate(picked, axis=1).astype(jnp.bfloat16)
+
+    def tok_copy(k):
+        dst = (me + k) % 8
+        return remote(contrib.at[dst], tokens.at[me], tok_send.at[dst], tok_recv.at[me], to(dst))
+
+    for k in range(1, 8):
+        tok_copy(k).start()
+
+    loads[1].wait()
+
+    def head_pair(p, carry):
+        cols = pl.ds(pl.multiple_of(p * 384, 128), 384)
+        both = jnp.concatenate([queries[0, :, cols].astype(jnp.float32), queries[1, :, cols].astype(jnp.float32)], axis=0)
+        for j in range(2):
+            h = p * 2 + j
+            nope = both[:, 192 * j : 192 * j + 128].astype(jnp.bfloat16)
+            rope = both[:, 192 * j + 128 : 192 * j + 192].astype(jnp.bfloat16)
+            rows = pl.ds(pl.multiple_of(h * 16, 16), 16)
+            q_all[rows, :512] = jnp.dot(nope, uk_v[h], preferred_element_type=jnp.float32).astype(jnp.bfloat16)
+            q_all[rows, 512:] = rope
+        return carry
+
+    lax.fori_loop(0, head_count // 2, head_pair, 0)
+
+    total = row_of.shape[0]
+    block_here = jnp.int32(0)
+    for b in range(8):
+        block_here = block_here + jnp.where(decode_perm[b] == me, b, 0)
+    sample = block_here * 8 + lax.broadcasted_iota(jnp.int32, (total, 128), 0) % 8
+    prompt = jnp.zeros((total, 128), jnp.int32)
+    ends = jnp.int32(0)
+    for p in range(prompts):
+        ends = ends + counts[p]
+        prompt = prompt + jnp.where(sample >= ends, 1, 0)
+    rows_vec = jnp.zeros((total, 128), jnp.int32)
+    for p in range(prompts):
+        rows_vec = jnp.where(prompt == p, prompt_rows[p], rows_vec)
+    row_of[...] = rows_vec
+    loads[2].wait()
+
+    score_scale = (NOPE_DIM + ROPE_DIM) ** (-0.5)
+
+    def begin():
+        fresh = contrib[me].astype(jnp.float32)
+        for k in range(1, 8):
+            src = (me + k) % 8
+            pltpu.make_async_copy(tokens.at[src], tokens.at[src], tok_recv.at[src]).wait()
+            fresh = fresh + tokens[src].astype(jnp.float32)
+        rope = fresh[:, 512:]
+        swap = lax.broadcasted_iota(jnp.int32, (64, 64), 0) == (lax.broadcasted_iota(jnp.int32, (64, 64), 1) + 32) % 64
+        swapped = jnp.dot(
+            rope.astype(jnp.bfloat16), jnp.where(swap, 1.0, 0.0).astype(jnp.bfloat16), preferred_element_type=jnp.float32
+        )
+        new_keys[:, :512] = fresh[:, :512].astype(jnp.bfloat16)
+        new_keys[:, 512:] = (rope * rope_cos[...] + swapped * rope_sin[...]).astype(jnp.bfloat16)
+        scores = contract_last(q_all[...], new_keys[...]) * score_scale
+        row = lax.broadcasted_iota(jnp.int32, (total, 16), 0) % 16
+        key = lax.broadcasted_iota(jnp.int32, (total, 16), 1)
+        seen = (row % 8 == key % 8) & (key // 8 <= row // 8)
+        scores = jnp.where(seen, scores, masked_fill)
+        top = jnp.max(scores, axis=1, keepdims=True)
+        probs = jnp.exp(scores - top)
+        m_ref[...] = jnp.broadcast_to(top, m_ref.shape)
+        l_ref[...] = jnp.broadcast_to(jnp.sum(probs, axis=1, keepdims=True), l_ref.shape)
+        acc[...] = jnp.dot(probs.astype(jnp.bfloat16), new_keys[:, :512], preferred_element_type=jnp.float32)
+
+    def attend(src):
+        keys = kv[src].reshape(prompts * block, kv.shape[-1])
+        scores = contract_last(q_all[...], keys)
+        rows = row_of[...]
+        chosen = scores[:, :block]
+        for r in range(1, prompts):
+            chosen = jnp.where(rows == r, scores[:, r * block : (r + 1) * block], chosen)
+        chosen = chosen * score_scale
+        before = m_ref[...]
+        top = jnp.maximum(before, jnp.max(chosen, axis=1, keepdims=True))
+        fade = jnp.exp(before - top)
+        probs = jnp.exp(chosen - top)
+        m_ref[...] = top
+        l_ref[...] = l_ref[...] * fade + jnp.sum(probs, axis=1, keepdims=True)
+        spread = jnp.concatenate([jnp.where(rows == r, probs, 0.0).astype(jnp.bfloat16) for r in range(prompts)], axis=1)
+        gained = jnp.dot(spread, keys[:, :512], preferred_element_type=jnp.float32)
+        acc[...] = acc[...] * jnp.concatenate([fade] * 4, axis=1) + gained
+
+    def turn(i, carry):
+        @pl.when(i <= last)
+        def _():
+            await_block(layer(i) * 2 + y, core)
+
+            @pl.when(z_goes_on(i))
+            def _():
+                z_copy(i).start()
+
+            y_copy(i).start()
+            sib_copy(i, y).start()
+
+        @pl.when(i <= last + 1)
+        def _():
+            await_block(layer(i - 1) * 2 + flip, core)
+            sib_copy(i - 1, flip).start()
+
+        @pl.when(i == 2)
+        def _():
+            begin()
+
+        @pl.when(i >= 2)
+        def _():
+            near_layer = layer(i - 2)
+
+            @pl.when(i > 2)
+            def _():
+                await_block(near_layer * 2 + y, 1 - core)
+
+            await_block(near_layer * 2 + flip, 1 - core)
+
+            def one(side, c):
+                attend(near_layer * 2 + side)
+                return c
+
+            lax.fori_loop(0, 2, one, 0)
+
+        return carry
+
+    lax.fori_loop(1, last + 3, turn, 0)
+
+    att[...] = (acc[...] / jnp.concatenate([l_ref[...]] * 4, axis=1)).astype(jnp.bfloat16)
+    loads[3].wait()
+
+    def up_value(h, carry):
+        got = jnp.dot(att[pl.ds(pl.multiple_of(h * 16, 16), 16), :], uv_v[h], preferred_element_type=jnp.float32)
+        heads_all[me, :, pl.ds(pl.multiple_of(h * 128, 128), 128)] = got.astype(jnp.bfloat16)
+        return carry
+
+    lax.fori_loop(0, head_count, up_value, 0)
+
+    def ho_copy(src, send, device):
+        return remote(heads_all.at[src], heads_all.at[src], send, ho_recv.at[src], device)
+
+    def ho_own(step):
+        return ho_copy(me, ho_own_send.at[0 if step < 0 else 1], to(me + 2 * step))
+
+    def ho_z(i):
+        step = jnp.where(layer(i) < z, 2, -2)
+        return ho_copy(layer(i) * 2 + y, ho_z_send.at[i], to(me + step))
+
+    def ho_y(i):
+        return ho_copy(layer(i) * 2 + y, ho_y_send.at[i], to(z * 2 + flip))
+
+    def await_heads(src):
+        pltpu.make_async_copy(heads_all.at[src], heads_all.at[src], ho_recv.at[src]).wait()
+
+    ho_y(0).start()
+
+    @pl.when(z < last)
+    def _():
+        ho_own(1).start()
+
+    @pl.when(z > 0)
+    def _():
+        ho_own(-1).start()
+
+    for i in range(1, last + 1):
+        await_heads(layer(i) * 2 + y)
+
+        @pl.when(z_goes_on(i))
+        def _():
+            ho_z(i).start()
+
+        ho_y(i).start()
+    for i in range(last + 1):
+        await_heads(layer(i) * 2 + flip)
+    loads[4].wait()
+
+    depth = 512
+    rows_out = part.shape[0]
+    part[...] = jnp.zeros_like(part)
+
+    def project(k, carry):
+        cols = pl.ds(pl.multiple_of(k * depth, depth), depth)
+        left = heads_all[:, :, cols].reshape(rows_out, depth)
+        part[...] += jnp.dot(left, wout_v[cols, :], preferred_element_type=jnp.float32)
+        return carry
+
+    lax.fori_loop(0, wout_v.shape[0] // depth, project, 0)
+
+    kept = rows_out // 2
+    swap_copy = remote(
+        part.at[pl.ds(pl.multiple_of((1 - core) * kept, kept), kept)], other, ex_sem.at[0], ex_sem.at[1], sibling
+    )
+    swap_copy.start()
+
+    own_y_copy().wait_send()
+    ho_y(0).wait_send()
+
+    @pl.when(z < last)
+    def _():
+        own_copy(1).wait_send()
+        ho_own(1).wait_send()
+
+    @pl.when(z > 0)
+    def _():
+        own_copy(-1).wait_send()
+        ho_own(-1).wait_send()
+
+    sib_copy(0, flip).wait_send()
+    for i in range(1, last + 1):
+
+        @pl.when(z_goes_on(i))
+        def _():
+            z_copy(i).wait_send()
+            ho_z(i).wait_send()
+
+        y_copy(i).wait_send()
+        ho_y(i).wait_send()
+        sib_copy(i, y).wait_send()
+        sib_copy(i, flip).wait_send()
+    for k in range(1, 8):
+        tok_copy(k).wait_send()
+    swap_copy.wait()
+    out[...] = part[pl.ds(pl.multiple_of(core * kept, kept), kept), :] + other[...]
+
+
+def rope_tables(first, step_count, slots):
+    half_dim = ROPE_DIM // 2
+    freqs = np.float32(rope_base) ** (-np.arange(half_dim, dtype=np.float32) / np.float32(half_dim))
+    angles = (first + np.arange(step_count)).astype(np.float32)[:, None] * freqs.astype(np.float32)[None, :]
+    cosine = np.cos(angles.astype(np.float64)).astype(np.float32)
+    sine = np.sin(angles.astype(np.float64)).astype(np.float32)
+    return (
+        np.repeat(np.concatenate([cosine, cosine], axis=1), slots, axis=0),
+        np.repeat(np.concatenate([-sine, sine], axis=1), slots, axis=0),
+    )
+
+
+def fused_shards(store, queries, table, w_uk, w_uv, w_out, counts, prompt_rows, decode_perm, token_ids):
+    roll_count = lax.axis_size("roll")
+    step_count, slots_dev = queries.shape[:2]
+    prompts, block, latent = store.shape
+    head_count = w_uk.shape[0]
+    rows_q = head_count * step_count * slots_dev
+    rows_out = roll_count * step_count * slots_dev
+    width = w_out.shape[1]
+    cos_rows, sin_rows = rope_tables(block * roll_count, step_count, slots_dev)
+    bf16, f32 = jnp.bfloat16, jnp.float32
+    smem = pl.BlockSpec(memory_space=pltpu.SMEM)
+    vmem = pl.BlockSpec(memory_space=pltpu.VMEM)
+    anywhere = pl.BlockSpec(memory_space=pl.ANY)
+    dma = pltpu.SemaphoreType.DMA
+    summed = pl.pallas_call(
+        fused_kernel,
+        out_shape=jax.ShapeDtypeStruct((rows_out // 2, width), f32),
+        in_specs=[smem, smem, smem, vmem, vmem, vmem, vmem] + [anywhere] * 5,
+        out_specs=vmem,
+        scratch_shapes=[
+            pltpu.VMEM((roll_count, prompts, block, latent), bf16),
+            pltpu.VMEM(table.shape, bf16),
+            pltpu.VMEM(w_uk.shape, bf16),
+            pltpu.VMEM(w_uv.shape, bf16),
+            pltpu.VMEM(w_out.shape, bf16),
+            pltpu.VMEM((roll_count, 16, latent), bf16),
+            pltpu.VMEM((roll_count, 16, latent), bf16),
+            pltpu.VMEM((16, latent), bf16),
+            pltpu.VMEM((rows_q, latent), bf16),
+            pltpu.VMEM((rows_q, 128), jnp.int32),
+            pltpu.VMEM((rows_q, 128), f32),
+            pltpu.VMEM((rows_q, 128), f32),
+            pltpu.VMEM((rows_q, KV_RANK), f32),
+            pltpu.VMEM((rows_q, KV_RANK), bf16),
+            pltpu.VMEM((roll_count, 16, w_out.shape[0]), bf16),
+            pltpu.VMEM((rows_out, width), f32),
+            pltpu.VMEM((rows_out // 2, width), f32),
+            dma((5,)), dma((8, 2)), dma((2,)), dma((4,)), dma((4,)), dma((4, 2)), dma((8,)), dma((8,)),
+            dma((8,)), dma((2,)), dma((4,)), dma((4,)), dma((2,)),
+        ],
+        compiler_params=pltpu.CompilerParams(
+            collective_id=0, has_side_effects=True, vmem_limit_bytes=56 * 1024 * 1024
+        ),
+        name="fused_attention",
+    )(
+        counts, prompt_rows, decode_perm, token_ids, jnp.asarray(cos_rows), jnp.asarray(sin_rows), queries, store, table,
+        w_uk, w_uv, w_out,
+    )
+    by_slot = summed.reshape(-1, step_count, slots_dev, width).transpose(0, 2, 1, 3)
+    return by_slot.reshape(-1, step_count, width).astype(bf16)
+
+
 def solution(mesh):
+    body = fused_shards if mesh.shape["roll"] == 8 and mesh.shape["head"] == 2 else shards
     in_specs = (
         P("grp", "roll", None),
         P(None, ("grp", "roll"), "head"),
@@ -131,4 +526,4 @@
         P("grp", None),
     )
     out_specs = P(("grp", "head"), None, "roll")
-    return jax.shard_map(shards, mesh=mesh, in_specs=in_specs, out_specs=out_specs, check_vma=False)
+    return jax.shard_map(body, mesh=mesh, in_specs=in_specs, out_specs=out_specs, check_vma=False)

time: 364 us -> 79.1 us (0.22)
  waiting for transfers between devices: 253 us -> 0 us
  Pallas kernels: 0 us -> 71.2 us
  local copies, waits for them, and re-layouts: 52.4 us -> 6.7 us
  matrix products: 22.4 us -> 0 us
  between operations: 13.3 us -> 0.01 us
  other arithmetic: 13.8 us -> 0.95 us
  starting transfers between devices: 7.53 us -> 0 us
    reduce_scatter x2 -> x0, waiting for transfers between devices: 215 us -> none  [the longest x1 208 us: shards(): lax.psum_scatter(jnp.dot(one_hot, table, preferred_element_type=jnp.float...]
    pallas_call x0 -> x1, Pallas kernels: none -> 71.2 us  [fused_shards(): pl.pallas_call(fused_kernel, out_shape=jax.ShapeDtypeStruct((rows_out //...]
    all_gather x1 -> x0, waiting for transfers between devices: 38.4 us -> none  [shards(): lax.all_gather(slot_major, 'roll', axis=0, tiled=True)]
    reshape x6 -> x0, local copies, waits for them, and re-layouts: 30.8 us -> none  [the longest x2 29.7 us: shards(): cache_rows = incoming.reshape(slots_dev, cache_len, latent_width)]
    dot_general x7 -> x0, matrix products: 19.5 us -> none  [the longest x1 5.85 us: shards(): jnp.einsum('tshc,sjc->tshj', q_full, cache_rows, preferred_element_type=j...]
    all_to_all x1 -> x0, local copies, waits for them, and re-layouts: 13.4 us -> none  [shards(): lax.all_to_all(outgoing, 'roll', split_axis=0, concat_axis=2, tiled=True)]
    select_n x2 -> x0, other arithmetic: 8.31 us -> none  [shards(): jnp.take(store, send_rows, axis=0)]
    all_to_all x1 -> x0, starting transfers between devices: 7.41 us -> none  [shards(): lax.all_to_all(outgoing, 'roll', split_axis=0, concat_axis=2, tiled=True)]
  transfers between devices with their start and end apart: 4 -> 0, of which waited for: 3 -> 0; matrix products, arithmetic and copies ran while one was open for 2% -> 0% of each run, Pallas kernels for 0% -> 0%
where the time goes in v1:
time: 79.1 us; the launch traced here: 78.9 us
  Pallas kernels  71.2 us (90%)
  local copies, waits for them, and re-layouts  6.7 us (8%)
  other arithmetic  0.95 us (1%)
    pallas_call x1, Pallas kernels, fused_shards(): pl.pallas_call(fused_kernel, out_shape=jax.ShapeDtypeStruct((rows_out //...  71.2 us
    unnamed x3, local copies, waits for them, and re-layouts  5.97 us

profile of v1, /device:TPU:0, one launch (start us, length us, event | category | flops | bytes accessed | tf_op | source)
XLA Modules:
  0.0 78.9 jit_solution(10791412535911430907)
XLA Ops:
  0.0 1.4 %copy.13.token_ids = s32[64,2]{1,0:T(8,128)} copy(s32[64,2]{0,1:T(2,128)} %param.21) | data formatting | bytes 1024 | tf_op args[9]
  1.4 2.2 %copy.14.store = bf16[4,128,576]{2,1,0:T(8,128)(2,1)} copy(bf16[4,128,576]{1,2,0:T(8,128)(2,1)} %param.12) | data formatting | bytes 1179648 | tf_op args[0]
  3.6 2.4 %copy.15.table = bf16[1024,576]{1,0:T(8,128)(2,1)} copy(bf16[1024,576]{0,1:T(8,128)(2,1)} %param.14) | data formatting | bytes 2359296 | tf_op args[2]
  6.0 71.2 %fused_attention.1 = f32[64,896]{1,0:T(8,128)} custom-call(s32[4]{0:T(128)} %counts.1, s32[4]{0:T(128)} %prompt_rows.1, s32[8]{0:T(128)} %decode_perm.1, s32[64,2]{1,0:T(8,128)} %copy.13.token_ids, f32[16,64]{1,0:T(8,128)} %constant.4.clone.rope_cos, f32[16,64]{1,0:T(8,128)} %constant.5.clone.rope_sin, bf16[2,8,6144]{2,1,0:T(8,128)(2,1)} %queries.1, ...), custom_call_target="tpu_custom_call" | custom-call | tf_op jit(solution)/shard_map/fused_attention/pallas_call | solution.py:476
  77.2 1.0 %convert_element_type.12 = bf16[64,896]{1,0:T(8,128)(2,1)S(1)} convert(f32[64,896]{1,0:T(8,128)} %fused_attention.1) | non-fusion elementwise | flops 57344 | bytes 344064 | tf_op jit(solution)/shard_map/convert_element_type | solution.py:511
  78.2 0.7 copy.16

commit v2 on v1

--- a/solution.py
+++ b/solution.py
@@ -139,7 +139,7 @@
     flip = 1 - y
     prompts = store.shape[0]
     half = prompts // 2
-    block = store.shape[1]
+    block = store.shape[2]
     head_count = uk_v.shape[0]
     last = 3
 
@@ -217,13 +217,13 @@
         own_copy(-1).start()
 
     loads[0].wait()
-    rows_here = table_v.shape[0]
-    spots = lax.broadcasted_iota(jnp.int32, (token_ids.shape[0], rows_here), 1) + me * rows_here
-    picked = []
-    for t in range(2):
-        hot = jnp.where(token_ids[:, t : t + 1] == spots, 1.0, 0.0).astype(jnp.bfloat16)
-        got = jnp.dot(hot, table_v[...], preferred_element_type=jnp.float32)
-        picked.append(got.reshape(8, 8, got.shape[-1]))
+    rows_here = table_v.shape[1]
+    slots = token_ids.shape[1]
+    ids = jnp.concatenate([token_ids[0:1, :], token_ids[1:2, :]], axis=1)
+    spots = lax.broadcasted_iota(jnp.int32, (rows_here, 2 * slots), 0) + me * rows_here
+    hot = jnp.where(ids == spots, 1.0, 0.0).astype(jnp.bfloat16)
+    got = jnp.dot(table_v[...], hot, preferred_element_type=jnp.float32)
+    picked = [got.T[t * slots : (t + 1) * slots].reshape(8, 8, got.shape[0]) for t in range(2)]
     contrib[...] = jnp.concatenate(picked, axis=1).astype(jnp.bfloat16)
 
     def tok_copy(k):
@@ -292,8 +292,8 @@
         acc[...] = jnp.dot(probs.astype(jnp.bfloat16), new_keys[:, :512], preferred_element_type=jnp.float32)
 
     def attend(src):
-        keys = kv[src].reshape(prompts * block, kv.shape[-1])
-        scores = contract_last(q_all[...], keys)
+        keys = jnp.concatenate([kv[src, r] for r in range(prompts)], axis=1)
+        scores = jnp.dot(q_all[...], keys, preferred_element_type=jnp.float32)
         rows = row_of[...]
         chosen = scores[:, :block]
         for r in range(1, prompts):
@@ -306,7 +306,7 @@
         m_ref[...] = top
         l_ref[...] = l_ref[...] * fade + jnp.sum(probs, axis=1, keepdims=True)
         spread = jnp.concatenate([jnp.where(rows == r, probs, 0.0).astype(jnp.bfloat16) for r in range(prompts)], axis=1)
-        gained = jnp.dot(spread, keys[:, :512], preferred_element_type=jnp.float32)
+        gained = contract_last(spread, keys[:512])
         acc[...] = acc[...] * jnp.concatenate([fade] * 4, axis=1) + gained
 
     def turn(i, carry):
@@ -444,7 +444,8 @@
     for k in range(1, 8):
         tok_copy(k).wait_send()
     swap_copy.wait()
-    out[...] = part[pl.ds(pl.multiple_of(core * kept, kept), kept), :] + other[...]
+    summed = part[pl.ds(pl.multiple_of(core * kept, kept), kept), :] + other[...]
+    out[...] = summed.astype(out.dtype)
 
 
 def rope_tables(first, step_count, slots):
@@ -475,12 +476,12 @@
     dma = pltpu.SemaphoreType.DMA
     summed = pl.pallas_call(
         fused_kernel,
-        out_shape=jax.ShapeDtypeStruct((rows_out // 2, width), f32),
+        out_shape=jax.ShapeDtypeStruct((rows_out // 2, width), bf16),
         in_specs=[smem, smem, smem, vmem, vmem, vmem, vmem] + [anywhere] * 5,
         out_specs=vmem,
         scratch_shapes=[
-            pltpu.VMEM((roll_count, prompts, block, latent), bf16),
-            pltpu.VMEM(table.shape, bf16),
+            pltpu.VMEM((roll_count, prompts, latent, block), bf16),
+            pltpu.VMEM((latent, table.shape[0]), bf16),
             pltpu.VMEM(w_uk.shape, bf16),
             pltpu.VMEM(w_uv.shape, bf16),
             pltpu.VMEM(w_out.shape, bf16),
@@ -504,11 +505,11 @@
         ),
         name="fused_attention",
     )(
-        counts, prompt_rows, decode_perm, token_ids, jnp.asarray(cos_rows), jnp.asarray(sin_rows), queries, store, table,
-        w_uk, w_uv, w_out,
+        counts, prompt_rows, decode_perm, token_ids.T, jnp.asarray(cos_rows), jnp.asarray(sin_rows), queries,
+        store.transpose(0, 2, 1), table.T, w_uk, w_uv, w_out,
     )
     by_slot = summed.reshape(-1, step_count, slots_dev, width).transpose(0, 2, 1, 3)
-    return by_slot.reshape(-1, step_count, width).astype(bf16)
+    return by_slot.reshape(-1, step_count, width)
 
 
 def solution(mesh):

time: 79.1 us -> 70 us (0.88)
  local copies, waits for them, and re-layouts: 6.7 us -> 1.63 us
  Pallas kernels: 71.2 us -> 68.3 us
  other arithmetic: 0.95 us -> 0 us
    unnamed x3 -> x0, local copies, waits for them, and re-layouts: 5.97 us -> none
    pallas_call x1, Pallas kernels: 71.2 us -> 68.3 us  [fused_shards(): pl.pallas_call(fused_kernel, out_shape=jax.ShapeDtypeStruct((rows_out //...]
    transpose x0 -> x1, local copies, waits for them, and re-layouts: none -> 1.63 us  [fused_shards(): summed.reshape(-1, step_count, slots_dev, width).transpose(0, 2, 1, 3)]
    convert_element_type x1 -> x0, other arithmetic: 0.95 us -> none  [fused_shards(): return by_slot.reshape(-1, step_count, width).astype(bf16)]
where the time goes in v2:
time: 70 us; the launch traced here: 69.9 us
  Pallas kernels  68.3 us (98%)
  local copies, waits for them, and re-layouts  1.63 us (2%)
    pallas_call x1, Pallas kernels, fused_shards(): pl.pallas_call(fused_kernel, out_shape=jax.ShapeDtypeStruct((rows_out //...  68.3 us
    transpose x1, local copies, waits for them, and re-layouts, fused_shards(): summed.reshape(-1, step_count, slots_dev, width).transpose(0, 2, 1, 3)  1.63 us

profile of v2, /device:TPU:0, one launch (start us, length us, event | category | flops | bytes accessed | tf_op | source)
XLA Modules:
  0.0 69.9 jit_solution(531400314357675525)
XLA Ops:
  0.0 68.3 %fused_attention.1 = bf16[64,896]{1,0:T(8,128)(2,1)} custom-call(s32[4]{0:T(128)} %counts.1, s32[4]{0:T(128)} %prompt_rows.1, s32[8]{0:T(128)} %decode_perm.1, s32[2,64]{1,0:T(2,128)} %bitcast.10, f32[16,64]{1,0:T(8,128)} %constant.4.clone.rope_cos, f32[16,64]{1,0:T(8,128)} %constant.5.clone.rope_sin, bf16[2,8,6144]{2,1,0:T(8,128)(2,1)} %queries.1, ...), custom_call_target="tpu_custom_call" | custom-call | tf_op jit(solution)/shard_map/fused_attention/pallas_call | solution.py:477
  68.3 1.6 %copy.13 = bf16[4,8,2,896]{3,2,1,0:T(2,128)(2,1)} copy(bf16[4,8,2,896]{3,1,2,0:T(8,128)(2,1)} %bitcast.9) | data formatting | bytes 229376 | tf_op jit(solution)/shard_map/transpose | solution.py:511

commit v3 on v2

--- a/solution.py
+++ b/solution.py
@@ -130,8 +130,8 @@
     counts, prompt_rows, decode_perm, token_ids, rope_cos, rope_sin, queries, store, table, w_uk, w_uv, w_out,
     out,
     kv, table_v, uk_v, uv_v, wout_v, contrib, tokens, new_keys, q_all, row_of, m_ref, l_ref, acc, att, heads_all, part, other,
-    load_sem, kv_recv, own_send, z_send, y_send, sib_send, tok_recv, tok_send,
-    ho_recv, ho_own_send, ho_z_send, ho_y_send, ex_sem,
+    load_sem, kv_recv, kv_own, kv_z, kv_y, sib_own, sib_z, sib_y, tok_recv, tok_send,
+    ho_recv, ho_own, ho_z, ho_y, ex_sem,
 ):
     me = lax.axis_index("roll")
     core = lax.axis_index("head")
@@ -147,8 +147,6 @@
         return {"roll": roll}
 
     sibling = {"head": 1 - core}
-    mine = pl.ds(half * core, half)
-
     def remote(src, dst, send, recv, device):
         return pltpu.make_async_remote_copy(
             src_ref=src, dst_ref=dst, send_sem=send, recv_sem=recv, device_id=device,
@@ -177,44 +175,158 @@
         up = jnp.where(i == 0, near, jnp.where(i > near, i, i - 1))
         return jnp.where(z <= 1, up, last - up)
 
-    own_block = store.at[mine]
-
-    def own_copy(step):
-        slot = 0 if step < 0 else 1
-        return remote(own_block, kv.at[me, mine], own_send.at[slot], kv_recv.at[me, core], to(me + 2 * step))
-
-    def z_copy(i):
-        src = layer(i) * 2 + y
-        step = jnp.where(layer(i) < z, 2, -2)
-        return remote(kv.at[src, mine], kv.at[src, mine], z_send.at[i], kv_recv.at[src, core], to(me + step))
-
-    def z_goes_on(i):
-        return jnp.where(layer(i) < z, z < last, z > 0)
-
-    def y_copy(i):
-        src = layer(i) * 2 + y
-        return remote(kv.at[src, mine], kv.at[src, mine], y_send.at[i], kv_recv.at[src, core], to(z * 2 + flip))
-
-    def own_y_copy():
-        return remote(own_block, kv.at[me, mine], y_send.at[0], kv_recv.at[me, core], to(z * 2 + flip))
-
-    def sib_copy(i, side):
-        src = layer(i) * 2 + side
-        return remote(kv.at[src, mine], kv.at[src, mine], sib_send.at[i, side], kv_recv.at[src, core], sibling)
-
-    def await_block(src, which):
-        ref = kv.at[src, pl.ds(half * which, half)]
-        pltpu.make_async_copy(ref, ref, kv_recv.at[src, which]).wait()
-
-    own_y_copy().start()
-
-    @pl.when(z < last)
-    def _():
-        own_copy(1).start()
-
-    @pl.when(z > 0)
-    def _():
-        own_copy(-1).start()
+    def from_side(side, t):
+        layers = z if side == 0 else last - z
+        extra = t == 2 * layers
+        away = jnp.minimum(t // 2, layers - 1) + 1
+        origin = jnp.where(extra, flip, y) + 2 * (z - away if side == 0 else z + away)
+        crossed = 2 * (z - away if side == 0 else z + away) + flip
+        comes = (layers > 0) & (t <= 2 * layers)
+        goes_on = comes & (z < last if side == 0 else z > 0)
+        return origin, jnp.where(extra, 1, t % 2), comes, goes_on, t < 2 * layers - 1, crossed
+
+    def onward(side):
+        return to(me + 2 if side == 0 else me - 2)
+
+    across = to(z * 2 + flip)
+
+    class Relay:
+        def __init__(self, piece, recv, own, along, over, swap=None):
+            self.piece, self.recv, self.own, self.along, self.over, self.swap = piece, recv, own, along, over, swap
+
+        def send(self, src, q, sem, device):
+            return remote(self.piece(src, q), self.piece(src, q), sem, self.recv(src, q), device)
+
+        def arrive(self, src, q):
+            ref = self.piece(src, q)
+            pltpu.make_async_copy(ref, ref, self.recv(src, q)).wait()
+
+        def mine(self, q, act):
+            act(self.send(me, q, self.own.at[2, q], across))
+            for side in range(2):
+
+                @pl.when(z < last if side == 0 else z > 0)
+                def _():
+                    act(self.send(me, q, self.own.at[side, q], onward(side)))
+
+        def end_extra(self, act):
+            for side in range(2):
+
+                @pl.when(z == 0 if side == 0 else z == last)
+                def _():
+                    act(self.send(z * 2 + flip, 1, self.own.at[3, side], onward(side)))
+
+        def along_turn(self, t):
+            for side in range(2):
+                src, q, comes, goes_on, crosses, _ = from_side(side, t)
+
+                @pl.when(comes)
+                def _():
+                    self.arrive(src, q)
+
+                    @pl.when(goes_on)
+                    def _():
+                        self.send(src, q, self.along.at[side, t], onward(side)).start()
+
+                    @pl.when(crosses)
+                    def _():
+                        self.send(src, q, self.over.at[side, t], across).start()
+
+                    if self.swap:
+                        self.send(src, q, self.swap[1].at[side, t], sibling).start()
+
+        def own_crossed(self, t):
+            self.arrive(z * 2 + flip, t)
+            if self.swap:
+                self.send(z * 2 + flip, t, self.swap[0].at[t], sibling).start()
+
+        def crossed_turn(self, t):
+            for side in range(2):
+                _, q, _, _, crosses, src = from_side(side, t)
+
+                @pl.when(crosses)
+                def _():
+                    self.arrive(src, q)
+                    if self.swap:
+                        self.send(src, q, self.swap[2].at[side, t], sibling).start()
+
+        def turn(self, t):
+            self.along_turn(t)
+
+            @pl.when(t < 2)
+            def _():
+                self.own_crossed(t)
+
+            @pl.when(t == 1)
+            def _():
+                self.end_extra(lambda c: c.start())
+
+            @pl.when(t >= 2)
+            def _():
+                self.crossed_turn(t - 2)
+
+        def settle(self):
+            def leave(c):
+                c.wait_send()
+
+            for q in range(2):
+                self.mine(q, leave)
+                if self.swap:
+                    leave(self.send(z * 2 + flip, q, self.swap[0].at[q], sibling))
+            self.end_extra(leave)
+
+            def one(t, carry):
+                for side in range(2):
+                    src, q, comes, goes_on, crosses, other_src = from_side(side, t)
+
+                    @pl.when(goes_on)
+                    def _():
+                        leave(self.send(src, q, self.along.at[side, t], onward(side)))
+
+                    @pl.when(crosses)
+                    def _():
+                        leave(self.send(src, q, self.over.at[side, t], across))
+
+                    if self.swap:
+
+                        @pl.when(comes)
+                        def _():
+                            leave(self.send(src, q, self.swap[1].at[side, t], sibling))
+
+                        @pl.when(crosses)
+                        def _():
+                            leave(self.send(other_src, q, self.swap[2].at[side, t], sibling))
+
+                return carry
+
+            lax.fori_loop(0, turns, one, 0)
+
+    turns = 7
+    cache = Relay(
+        lambda src, q: kv.at[src, half * core + q],
+        lambda src, q: kv_recv.at[src, half * core + q],
+        kv_own, kv_z, kv_y, (sib_own, sib_z, sib_y),
+    )
+
+    def await_sibling(src):
+        for q in range(half):
+            r = half * (1 - core) + q
+            pltpu.make_async_copy(kv.at[src, r], kv.at[src, r], kv_recv.at[src, r]).wait()
+
+    def send_own_cache(q, act):
+        own = store.at[half * core + q]
+        here = kv.at[me, half * core + q]
+        sem = kv_recv.at[me, half * core + q]
+        act(remote(own, here, kv_own.at[2, q], sem, across))
+        for side in range(2):
+
+            @pl.when(z < last if side == 0 else z > 0)
+            def _():
+                act(remote(own, here, kv_own.at[side, q], sem, onward(side)))
+
+    cache.mine = send_own_cache
+    for q in range(2):
+        cache.mine(q, lambda c: c.start())
 
     loads[0].wait()
     rows_here = table_v.shape[1]
@@ -246,8 +358,6 @@
             q_all[rows, :512] = jnp.dot(nope, uk_v[h], preferred_element_type=jnp.float32).astype(jnp.bfloat16)
             q_all[rows, 512:] = rope
         return carry
-
-    lax.fori_loop(0, head_count // 2, head_pair, 0)
 
     total = row_of.shape[0]
     block_here = jnp.int32(0)
@@ -309,103 +419,74 @@
         gained = contract_last(spread, keys[:512])
         acc[...] = acc[...] * jnp.concatenate([fade] * 4, axis=1) + gained
 
-    def turn(i, carry):
-        @pl.when(i <= last)
+    def gather_turn(t, carry):
+        cache.turn(t)
+
+        @pl.when(t < 2)
         def _():
-            await_block(layer(i) * 2 + y, core)
-
-            @pl.when(z_goes_on(i))
-            def _():
-                z_copy(i).start()
-
-            y_copy(i).start()
-            sib_copy(i, y).start()
-
-        @pl.when(i <= last + 1)
-        def _():
-            await_block(layer(i - 1) * 2 + flip, core)
-            sib_copy(i - 1, flip).start()
-
-        @pl.when(i == 2)
+            pairs = head_count // 4
+            lax.fori_loop(t * pairs, t * pairs + pairs, head_pair, 0)
+
+        @pl.when(t == 2)
         def _():
             begin()
 
-        @pl.when(i >= 2)
+        def one(j, c):
+            k = 2 * t - 5 + j
+
+            @pl.when((k >= 0) & (k < 8))
+            def _():
+                src = 2 * layer(k // 2) + jnp.where(k % 2 == 0, y, flip)
+
+                @pl.when(k > 0)
+                def _():
+                    await_sibling(src)
+
+                attend(src)
+
+            return c
+
+        @pl.when(t >= 2)
         def _():
-            near_layer = layer(i - 2)
-
-            @pl.when(i > 2)
-            def _():
-                await_block(near_layer * 2 + y, 1 - core)
-
-            await_block(near_layer * 2 + flip, 1 - core)
-
-            def one(side, c):
-                attend(near_layer * 2 + side)
-                return c
-
             lax.fori_loop(0, 2, one, 0)
 
         return carry
 
-    lax.fori_loop(1, last + 3, turn, 0)
+    lax.fori_loop(0, turns, gather_turn, 0)
 
     att[...] = (acc[...] / jnp.concatenate([l_ref[...]] * 4, axis=1)).astype(jnp.bfloat16)
     loads[3].wait()
 
+    per_piece = head_count // 2
+
     def up_value(h, carry):
         got = jnp.dot(att[pl.ds(pl.multiple_of(h * 16, 16), 16), :], uv_v[h], preferred_element_type=jnp.float32)
-        heads_all[me, :, pl.ds(pl.multiple_of(h * 128, 128), 128)] = got.astype(jnp.bfloat16)
+        spot = h % per_piece
+        heads_all[h // per_piece, me, :, pl.ds(pl.multiple_of(spot * 128, 128), 128)] = got.astype(jnp.bfloat16)
         return carry
 
-    lax.fori_loop(0, head_count, up_value, 0)
-
-    def ho_copy(src, send, device):
-        return remote(heads_all.at[src], heads_all.at[src], send, ho_recv.at[src], device)
-
-    def ho_own(step):
-        return ho_copy(me, ho_own_send.at[0 if step < 0 else 1], to(me + 2 * step))
-
-    def ho_z(i):
-        step = jnp.where(layer(i) < z, 2, -2)
-        return ho_copy(layer(i) * 2 + y, ho_z_send.at[i], to(me + step))
-
-    def ho_y(i):
-        return ho_copy(layer(i) * 2 + y, ho_y_send.at[i], to(z * 2 + flip))
-
-    def await_heads(src):
-        pltpu.make_async_copy(heads_all.at[src], heads_all.at[src], ho_recv.at[src]).wait()
-
-    ho_y(0).start()
-
-    @pl.when(z < last)
-    def _():
-        ho_own(1).start()
-
-    @pl.when(z > 0)
-    def _():
-        ho_own(-1).start()
-
-    for i in range(1, last + 1):
-        await_heads(layer(i) * 2 + y)
-
-        @pl.when(z_goes_on(i))
-        def _():
-            ho_z(i).start()
-
-        ho_y(i).start()
-    for i in range(last + 1):
-        await_heads(layer(i) * 2 + flip)
+    shared = Relay(lambda src, q: heads_all.at[q, src], lambda src, q: ho_recv.at[src, q], ho_own, ho_z, ho_y)
+    for q in range(2):
+        lax.fori_loop(q * per_piece, (q + 1) * per_piece, up_value, 0)
+        shared.mine(q, lambda c: c.start())
+
+    def share_turn(t, carry):
+        shared.turn(t)
+        return carry
+
+    lax.fori_loop(0, turns, share_turn, 0)
     loads[4].wait()
 
     depth = 512
     rows_out = part.shape[0]
     part[...] = jnp.zeros_like(part)
+    per_half = wout_v.shape[0] // 2 // depth
 
     def project(k, carry):
-        cols = pl.ds(pl.multiple_of(k * depth, depth), depth)
-        left = heads_all[:, :, cols].reshape(rows_out, depth)
-        part[...] += jnp.dot(left, wout_v[cols, :], preferred_element_type=jnp.float32)
+        cols = pl.ds(pl.multiple_of((k % per_half) * depth, depth), depth)
+        left = heads_all[k // per_half, :, :, cols].reshape(rows_out, depth)
+        rows = pl.ds(pl.multiple_of(k * depth, depth), depth)
+        part[...] += jnp.dot(left, wout_v[rows, :], preferred_element_type=jnp.float32)
         return carry
 
     lax.fori_loop(0, wout_v.shape[0] // depth, project, 0)
@@ -416,31 +497,8 @@
     )
     swap_copy.start()
 
-    own_y_copy().wait_send()
-    ho_y(0).wait_send()
-
-    @pl.when(z < last)
-    def _():
-        own_copy(1).wait_send()
-        ho_own(1).wait_send()
-
-    @pl.when(z > 0)
-    def _():
-        own_copy(-1).wait_send()
-        ho_own(-1).wait_send()
-
-    sib_copy(0, flip).wait_send()
-    for i in range(1, last + 1):
-
-        @pl.when(z_goes_on(i))
-        def _():
-            z_copy(i).wait_send()
-            ho_z(i).wait_send()
-
-        y_copy(i).wait_send()
-        ho_y(i).wait_send()
-        sib_copy(i, y).wait_send()
-        sib_copy(i, flip).wait_send()
+    cache.settle()
+    shared.settle()
     for k in range(1, 8):
         tok_copy(k).wait_send()
     swap_copy.wait()
@@ -494,11 +552,11 @@
             pltpu.VMEM((rows_q, 128), f32),
             pltpu.VMEM((rows_q, KV_RANK), f32),
             pltpu.VMEM((rows_q, KV_RANK), bf16),
-            pltpu.VMEM((roll_count, 16, w_out.shape[0]), bf16),
+            pltpu.VMEM((2, roll_count, 16, w_out.shape[0] // 2), bf16),
             pltpu.VMEM((rows_out, width), f32),
             pltpu.VMEM((rows_out // 2, width), f32),
-            dma((5,)), dma((8, 2)), dma((2,)), dma((4,)), dma((4,)), dma((4, 2)), dma((8,)), dma((8,)),
-            dma((8,)), dma((2,)), dma((4,)), dma((4,)), dma((2,)),
+            dma((5,)), dma((8, 4)), dma((4, 2)), dma((2, 7)), dma((2, 7)), dma((2,)), dma((2, 7)), dma((2, 7)),
+            dma((8,)), dma((8,)), dma((8, 2)), dma((4, 2)), dma((2, 7)), dma((2, 7)), dma((2,)),
         ],
         compiler_params=pltpu.CompilerParams(
             collective_id=0, has_side_effects=True, vmem_limit_bytes=56 * 1024 * 1024

time: 70 us -> 62.5 us (0.89)
  Pallas kernels: 68.3 us -> 60.7 us
    pallas_call x1, Pallas kernels: 68.3 us -> 60.7 us  [fused_shards(): pl.pallas_call(fused_kernel, out_shape=jax.ShapeDtypeStruct((rows_out //...]
where the time goes in v3:
time: 62.5 us; the launch traced here: 62.4 us
  Pallas kernels  60.7 us (97%)
  local copies, waits for them, and re-layouts  1.63 us (3%)
    pallas_call x1, Pallas kernels, fused_shards(): pl.pallas_call(fused_kernel, out_shape=jax.ShapeDtypeStruct((rows_out //...  60.7 us
    transpose x1, local copies, waits for them, and re-layouts, fused_shards(): summed.reshape(-1, step_count, slots_dev, width).transpose(0, 2, 1, 3)  1.63 us

profile of v3, /device:TPU:0, one launch (start us, length us, event | category | flops | bytes accessed | tf_op | source)
XLA Modules:
  0.0 62.4 jit_solution(10531819253151005813)
XLA Ops:
  0.0 60.7 %fused_attention.1 = bf16[64,896]{1,0:T(8,128)(2,1)} custom-call(s32[4]{0:T(128)} %counts.1, s32[4]{0:T(128)} %prompt_rows.1, s32[8]{0:T(128)} %decode_perm.1, s32[2,64]{1,0:T(2,128)} %bitcast.10, f32[16,64]{1,0:T(8,128)} %constant.4.clone.rope_cos, f32[16,64]{1,0:T(8,128)} %constant.5.clone.rope_sin, bf16[2,8,6144]{2,1,0:T(8,128)(2,1)} %queries.1, ...), custom_call_target="tpu_custom_call" | custom-call | tf_op jit(solution)/shard_map/fused_attention/pallas_call | solution.py:535
  60.7 1.6 %copy.13 = bf16[4,8,2,896]{3,2,1,0:T(2,128)(2,1)} copy(bf16[4,8,2,896]{3,1,2,0:T(8,128)(2,1)} %bitcast.9) | data formatting | bytes 229376 | tf_op jit(solution)/shard_map/transpose | solution.py:569

commit v4 on v3

--- a/solution.py
+++ b/solution.py
@@ -129,7 +129,7 @@
 def fused_kernel(
     counts, prompt_rows, decode_perm, token_ids, rope_cos, rope_sin, queries, store, table, w_uk, w_uv, w_out,
     out,
-    kv, table_v, uk_v, uv_v, wout_v, contrib, tokens, new_keys, q_all, row_of, m_ref, l_ref, acc, att, heads_all, part, other,
+    kv, table_v, uk_v, uv_v, wout_v, contrib, tokens, tok_in, tok_out, new_keys, q_all, row_of, m_ref, l_ref, acc, att, heads_all, part, other,
     load_sem, kv_recv, kv_own, kv_z, kv_y, sib_own, sib_z, sib_y, tok_recv, tok_send,
     ho_recv, ho_own, ho_z, ho_y, ex_sem,
 ):
@@ -164,10 +164,21 @@
         load.start()
 
     barrier = pltpu.get_barrier_semaphore()
-    for k in range(1, 8):
-        pl.semaphore_signal(barrier, inc=1, device_id=to((me + k) % 8), device_id_type=pl.DeviceIdType.MESH)
-    pl.semaphore_signal(barrier, inc=1, device_id=sibling, device_id_type=pl.DeviceIdType.MESH)
-    pl.semaphore_wait(barrier, 8)
+    def greet(device):
+        pl.semaphore_signal(barrier, inc=1, device_id=device, device_id_type=pl.DeviceIdType.MESH)
+
+    greet(to(z * 2 + flip))
+    greet(sibling)
+
+    @pl.when(z < last)
+    def _():
+        greet(to(me + 2))
+
+    @pl.when(z > 0)
+    def _():
+        greet(to(me - 2))
+
+    pl.semaphore_wait(barrier, 2 + jnp.where(z < last, 1, 0) + jnp.where(z > 0, 1, 0))
 
     near = jnp.minimum(z, last - z)
 
@@ -336,14 +347,47 @@
     hot = jnp.where(ids == spots, 1.0, 0.0).astype(jnp.bfloat16)
     got = jnp.dot(table_v[...], hot, preferred_element_type=jnp.float32)
     picked = [got.T[t * slots : (t + 1) * slots].reshape(8, 8, got.shape[0]) for t in range(2)]
-    contrib[...] = jnp.concatenate(picked, axis=1).astype(jnp.bfloat16)
-
-    def tok_copy(k):
-        dst = (me + k) % 8
-        return remote(contrib.at[dst], tokens.at[me], tok_send.at[dst], tok_recv.at[me], to(dst))
-
-    for k in range(1, 8):
-        tok_copy(k).start()
+    both_steps = jnp.concatenate(picked, axis=1).astype(jnp.bfloat16)
+    for dst in range(8):
+        contrib[dst % 2, dst // 2] = both_steps[dst]
+
+    def tok_across():
+        return remote(contrib.at[flip], tok_in.at[2], tok_send.at[2], tok_recv.at[2], across)
+
+    def tok_along(side):
+        return remote(tok_out.at[side], tok_in.at[side], tok_send.at[side], tok_recv.at[side], onward(side))
+
+    def tok_await(side):
+        pltpu.make_async_copy(tok_in.at[side], tok_in.at[side], tok_recv.at[side]).wait()
+
+    tok_across().start()
+
+    def plus(a, b):
+        return (a.astype(jnp.float32) + b.astype(jnp.float32)).astype(jnp.bfloat16)
+
+    def token_turn(t):
+        @pl.when(t == 0)
+        def _():
+            tok_await(2)
+            tokens[...] = plus(contrib[y], tok_in[2])
+
+        for side in range(2):
+            place = z if side == 0 else last - z
+
+            @pl.when(place == t)
+            def _():
+                @pl.when(t > 0)
+                def _():
+                    tok_await(side)
+                    tok_out[side] = plus(tokens[...], tok_in[side])
+
+                @pl.when(t == 0)
+                def _():
+                    tok_out[side] = tokens[...]
+
+                @pl.when(t < last)
+                def _():
+                    tok_along(side).start()
 
     loads[1].wait()
 
@@ -373,16 +417,17 @@
     for p in range(prompts):
         rows_vec = jnp.where(prompt == p, prompt_rows[p], rows_vec)
     row_of[...] = rows_vec
+    m_ref[...] = jnp.full_like(m_ref, masked_fill)
+    l_ref[...] = jnp.zeros_like(l_ref)
+    acc[...] = jnp.zeros_like(acc)
     loads[2].wait()
 
     score_scale = (NOPE_DIM + ROPE_DIM) ** (-0.5)
 
-    def begin():
-        fresh = contrib[me].astype(jnp.float32)
-        for k in range(1, 8):
-            src = (me + k) % 8
-            pltpu.make_async_copy(tokens.at[src], tokens.at[src], tok_recv.at[src]).wait()
-            fresh = fresh + tokens[src].astype(jnp.float32)
+    def add_new():
+        fresh = (
+            tok_out[0, z].astype(jnp.float32) + tok_out[1, z].astype(jnp.float32) - tokens[z].astype(jnp.float32)
+        )
         rope = fresh[:, 512:]
         swap = lax.broadcasted_iota(jnp.int32, (64, 64), 0) == (lax.broadcasted_iota(jnp.int32, (64, 64), 1) + 32) % 64
         swapped = jnp.dot(
@@ -395,11 +440,14 @@
         key = lax.broadcasted_iota(jnp.int32, (total, 16), 1)
         seen = (row % 8 == key % 8) & (key // 8 <= row // 8)
         scores = jnp.where(seen, scores, masked_fill)
-        top = jnp.max(scores, axis=1, keepdims=True)
-        probs = jnp.exp(scores - top)
-        m_ref[...] = jnp.broadcast_to(top, m_ref.shape)
-        l_ref[...] = jnp.broadcast_to(jnp.sum(probs, axis=1, keepdims=True), l_ref.shape)
-        acc[...] = jnp.dot(probs.astype(jnp.bfloat16), new_keys[:, :512], preferred_element_type=jnp.float32)
+        before = m_ref[...]
+        top = jnp.maximum(before, jnp.max(scores, axis=1, keepdims=True))
+        fade = jnp.exp(before - top)
+        probs = jnp.exp(scores - top[:, :16])
+        m_ref[...] = top
+        l_ref[...] = l_ref[...] * fade + jnp.sum(probs, axis=1, keepdims=True)
+        gained = jnp.dot(probs.astype(jnp.bfloat16), new_keys[:, :512], preferred_element_type=jnp.float32)
+        acc[...] = acc[...] * jnp.concatenate([fade] * 4, axis=1) + gained
 
     def attend(src):
         keys = jnp.concatenate([kv[src, r] for r in range(prompts)], axis=1)
@@ -427,9 +475,13 @@
             pairs = head_count // 4
             lax.fori_loop(t * pairs, t * pairs + pairs, head_pair, 0)
 
-        @pl.when(t == 2)
+        @pl.when(t <= last)
         def _():
-            begin()
+            token_turn(t)
+
+        @pl.when(t == last + 1)
+        def _():
+            add_new()
 
         def one(j, c):
             k = 2 * t - 5 + j
@@ -454,20 +506,25 @@
 
     lax.fori_loop(0, turns, gather_turn, 0)
 
-    att[...] = (acc[...] / jnp.concatenate([l_ref[...]] * 4, axis=1)).astype(jnp.bfloat16)
+    att[...] = (acc[...] * jnp.concatenate([1.0 / l_ref[...]] * 4, axis=1)).astype(jnp.bfloat16)
     loads[3].wait()
 
     per_piece = head_count // 2
 
-    def up_value(h, carry):
-        got = jnp.dot(att[pl.ds(pl.multiple_of(h * 16, 16), 16), :], uv_v[h], preferred_element_type=jnp.float32)
-        spot = h % per_piece
-        heads_all[h // per_piece, me, :, pl.ds(pl.multiple_of(spot * 128, 128), 128)] = got.astype(jnp.bfloat16)
+    def up_value(step, carry):
+        got = []
+        for j in range(4):
+            h = step * 4 + j
+            rows = pl.ds(pl.multiple_of(h * 16, 16), 16)
+            got.append(jnp.dot(att[rows, :], uv_v[h], preferred_element_type=jnp.float32))
+        spot = (step * 4) % per_piece
+        wide = jnp.concatenate(got, axis=1).astype(jnp.bfloat16)
+        heads_all[step * 4 // per_piece, me, :, pl.ds(pl.multiple_of(spot * 128, 128), 512)] = wide
         return carry
 
     shared = Relay(lambda src, q: heads_all.at[q, src], lambda src, q: ho_recv.at[src, q], ho_own, ho_z, ho_y)
     for q in range(2):
-        lax.fori_loop(q * per_piece, (q + 1) * per_piece, up_value, 0)
+        lax.fori_loop(q * per_piece // 4, (q + 1) * per_piece // 4, up_value, 0)
         shared.mine(q, lambda c: c.start())
 
     def share_turn(t, carry):
@@ -499,8 +556,16 @@
 
     cache.settle()
     shared.settle()
-    for k in range(1, 8):
-        tok_copy(k).wait_send()
+    tok_across().wait_send()
+
+    @pl.when(z < last)
+    def _():
+        tok_along(0).wait_send()
+
+    @pl.when(z > 0)
+    def _():
+        tok_along(1).wait_send()
+
     swap_copy.wait()
     summed = part[pl.ds(pl.multiple_of(core * kept, kept), kept), :] + other[...]
     out[...] = summed.astype(out.dtype)
@@ -543,8 +608,10 @@
             pltpu.VMEM(w_uk.shape, bf16),
             pltpu.VMEM(w_uv.shape, bf16),
             pltpu.VMEM(w_out.shape, bf16),
-            pltpu.VMEM((roll_count, 16, latent), bf16),
-            pltpu.VMEM((roll_count, 16, latent), bf16),
+            pltpu.VMEM((2, roll_count // 2, 16, latent), bf16),
+            pltpu.VMEM((roll_count // 2, 16, latent), bf16),
+            pltpu.VMEM((3, roll_count // 2, 16, latent), bf16),
+            pltpu.VMEM((2, roll_count // 2, 16, latent), bf16),
             pltpu.VMEM((16, latent), bf16),
             pltpu.VMEM((rows_q, latent), bf16),
             pltpu.VMEM((rows_q, 128), jnp.int32),
@@ -556,7 +623,7 @@
             pltpu.VMEM((rows_out, width), f32),
             pltpu.VMEM((rows_out // 2, width), f32),
             dma((5,)), dma((8, 4)), dma((4, 2)), dma((2, 7)), dma((2, 7)), dma((2,)), dma((2, 7)), dma((2, 7)),
-            dma((8,)), dma((8,)), dma((8, 2)), dma((4, 2)), dma((2, 7)), dma((2, 7)), dma((2,)),
+            dma((3,)), dma((3,)), dma((8, 2)), dma((4, 2)), dma((2, 7)), dma((2, 7)), dma((2,)),
         ],
         compiler_params=pltpu.CompilerParams(
             collective_id=0, has_side_effects=True, vmem_limit_bytes=56 * 1024 * 1024

time: 62.5 us -> 62.6 us (level)
  no operation moved by 1% of the time
where the time goes in v4:
time: 62.6 us; the launch traced here: 62.5 us
  Pallas kernels  60.8 us (97%)
  local copies, waits for them, and re-layouts  1.63 us (3%)
    pallas_call x1, Pallas kernels, fused_shards(): pl.pallas_call(fused_kernel, out_shape=jax.ShapeDtypeStruct((rows_out //...  60.8 us
    transpose x1, local copies, waits for them, and re-layouts, fused_shards(): summed.reshape(-1, step_count, slots_dev, width).transpose(0, 2, 1, 3)  1.63 us

profile of v4, /device:TPU:0, one launch (start us, length us, event | category | flops | bytes accessed | tf_op | source)
XLA Modules:
  0.0 62.5 jit_solution(472412026761529860)
XLA Ops:
  0.0 60.8 %fused_attention.1 = bf16[64,896]{1,0:T(8,128)(2,1)} custom-call(s32[4]{0:T(128)} %counts.1, s32[4]{0:T(128)} %prompt_rows.1, s32[8]{0:T(128)} %decode_perm.1, s32[2,64]{1,0:T(2,128)} %bitcast.10, f32[16,64]{1,0:T(8,128)} %constant.4.clone.rope_cos, f32[16,64]{1,0:T(8,128)} %constant.5.clone.rope_sin, bf16[2,8,6144]{2,1,0:T(8,128)(2,1)} %queries.1, ...), custom_call_target="tpu_custom_call" | custom-call | tf_op jit(solution)/shard_map/fused_attention/pallas_call | solution.py:600
  60.8 1.6 %copy.13 = bf16[4,8,2,896]{3,2,1,0:T(2,128)(2,1)} copy(bf16[4,8,2,896]{3,1,2,0:T(8,128)(2,1)} %bitcast.9) | data formatting | bytes 229376 | tf_op jit(solution)/shard_map/transpose | solution.py:636

commit v5 on v4

--- a/solution.py
+++ b/solution.py
@@ -468,6 +468,10 @@
         acc[...] = acc[...] * jnp.concatenate([fade] * 4, axis=1) + gained
 
     def gather_turn(t, carry):
+        @pl.when(t == turns - 1)
+        def _():
+            add_new()
+
         cache.turn(t)
 
         @pl.when(t < 2)
@@ -475,14 +479,6 @@
             pairs = head_count // 4
             lax.fori_loop(t * pairs, t * pairs + pairs, head_pair, 0)
 
-        @pl.when(t <= last)
-        def _():
-            token_turn(t)
-
-        @pl.when(t == last + 1)
-        def _():
-            add_new()
-
         def one(j, c):
             k = 2 * t - 5 + j
 
@@ -501,6 +497,10 @@
         @pl.when(t >= 2)
         def _():
             lax.fori_loop(0, 2, one, 0)
+
+        @pl.when((t == 1) | ((t >= 3) & (t <= 5)))
+        def _():
+            token_turn(jnp.where(t == 1, 0, t - 2))
 
         return carry
 

time: 62.6 us -> 60.8 us (0.971)
  Pallas kernels: 60.8 us -> 59 us
    pallas_call x1, Pallas kernels: 60.8 us -> 59 us  [fused_shards(): pl.pallas_call(fused_kernel, out_shape=jax.ShapeDtypeStruct((rows_out //...]
where the time goes in v5:
time: 60.8 us; the launch traced here: 60.6 us
  Pallas kernels  59 us (97%)
  local copies, waits for them, and re-layouts  1.63 us (3%)
    pallas_call x1, Pallas kernels, fused_shards(): pl.pallas_call(fused_kernel, out_shape=jax.ShapeDtypeStruct((rows_out //...  59 us
    transpose x1, local copies, waits for them, and re-layouts, fused_shards(): summed.reshape(-1, step_count, slots_dev, width).transpose(0, 2, 1, 3)  1.63 us

profile of v5, /device:TPU:0, one launch (start us, length us, event | category | flops | bytes accessed | tf_op | source)
XLA Modules:
  0.0 60.6 jit_solution(7858647889685281910)
XLA Ops:
  0.0 59.0 %fused_attention.1 = bf16[64,896]{1,0:T(8,128)(2,1)} custom-call(s32[4]{0:T(128)} %counts.1, s32[4]{0:T(128)} %prompt_rows.1, s32[8]{0:T(128)} %decode_perm.1, s32[2,64]{1,0:T(2,128)} %bitcast.10, f32[16,64]{1,0:T(8,128)} %constant.4.clone.rope_cos, f32[16,64]{1,0:T(8,128)} %constant.5.clone.rope_sin, bf16[2,8,6144]{2,1,0:T(8,128)(2,1)} %queries.1, ...), custom_call_target="tpu_custom_call" | custom-call | tf_op jit(solution)/shard_map/fused_attention/pallas_call | solution.py:600
  59.0 1.6 %copy.13 = bf16[4,8,2,896]{3,2,1,0:T(2,128)(2,1)} copy(bf16[4,8,2,896]{3,1,2,0:T(8,128)(2,1)} %bitcast.9) | data formatting | bytes 229376 | tf_op jit(solution)/shard_map/transpose | solution.py:636
